TPU v7x, 32 devices: a whole 2x2x4 slice. The times are simulated.
32 devices in a mesh: groups: 2 (over x), ctx: 16 (over z, y, core).
Axes of the slice: x: 2, y: 2, z: 4, core: 2. Of those that a mesh axis runs over, the one named last changes fastest.
Arguments:
- mr_qkv: bfloat16 [16384, 12288], P(('groups', 'ctx')), parts along dimension 0, may hold values from -6 to 6
- mr_filter: bfloat16 [256, 128], replicated, may hold values from -0.5 to 0.5
- li_gates: bfloat16 [16384, 8192], P(('groups', 'ctx')), parts along dimension 0, may hold values from -6 to 6
- decay: float32 [4096, 16], replicated, may hold values from 2.4414063e-05 to 0.0333333333
- residue: float32 [4096, 16], replicated, may hold values from -1.8144368 to 1.8144368
Outputs:
- mixer_out: bfloat16 [16384, 4096], P(('groups', 'ctx')), parts along dimension 0
There are 2 independent parts, one for each index of `groups`. A program takes and returns all parts, laid end to end along the dimension named above; an argument that names none is the same for every part. Nothing has to cross between parts.
All inputs are finite; a program needn't handle non-finite values.
Results may differ from a plain program's by a relative error of at most 0.005.
Values may be sent and summed in bfloat16 or wider, within the bound.
A program may use at most 384 MiB of HBM per device.

v0:
```python
import functools

import jax
import jax.numpy as jnp
import numpy as np
from jax import lax
from jax.experimental import pallas as pl
from jax.experimental.pallas import tpu as pltpu
from jax.sharding import PartitionSpec as P

F32 = jnp.float32
BF16 = jnp.bfloat16
LEN = 128
NODES = 16
FAR_NODES = 32


def halves(table):
    high = table.astype(BF16)
    low = (table - high.astype(np.float64)).astype(BF16)
    return high, low


def lagrange(length, count):
    angle = (2 * np.arange(count) + 1) * np.pi / (2 * count)
    unit = np.cos(angle)
    weight = (-1.0) ** np.arange(count) * np.sin(angle)
    middle = (length - 1) / 2
    points = (np.arange(length) - middle) / middle
    gap = points[:, None] - unit[None, :]
    hit = np.abs(gap) < 1e-14
    ratio = weight[None, :] / np.where(hit, 1.0, gap)
    basis = ratio / ratio.sum(axis=1, keepdims=True)
    rows = hit.any(axis=1)
    basis[rows] = hit[rows]
    return middle + middle * unit, basis


def tables(width):
    freq = np.concatenate([np.arange(0, LEN, 2), np.arange(1, LEN, 2)])
    theta = np.pi * (freq[:, None] + 0.5) * np.arange(LEN)[None, :] / LEN
    forward = np.concatenate([np.cos(theta), -np.sin(theta)], axis=0)
    inverse = (forward.T / LEN).astype(BF16)
    nodes, basis = lagrange(LEN, NODES)
    fwd = np.concatenate([forward, basis[::-1].T], axis=0)
    fwd = np.concatenate(halves(fwd), axis=1)
    tap_high, tap_low = halves(forward @ basis)
    taps = np.concatenate([tap_high, tap_low, tap_high], axis=1)
    near_high, near_low = halves(basis)
    near = np.concatenate([near_high, near_low, near_high], axis=1)
    group = np.arange(width)[None, :] // 16 == np.arange(width // 16)[:, None]
    return nodes, fwd, inverse, taps, near, group


def dot(a, b):
    return lax.dot_general(a, b, (((1,), (0,)), ((), ())), preferred_element_type=F32)


def tripled(values):
    high = values.astype(BF16)
    low = (values - high.astype(F32)).astype(BF16)
    return jnp.concatenate([high, high, low], axis=0)


def twice(values):
    return jnp.concatenate([values, values], axis=0)


def times(re, im, filter_re, filter_im):
    return jnp.concatenate(
        [
            (re * filter_re - im * filter_im).astype(BF16),
            (re * filter_im + im * filter_re).astype(BF16),
        ],
        axis=0,
    )


def column(values):
    rows = lax.broadcasted_iota(jnp.int32, (len(values), 1), 0)
    total = jnp.zeros((len(values), 1), F32)
    for k, value in enumerate(values):
        total = jnp.where(rows == k, np.float32(value), total)
    return total


def near_kernel(
    nodes, q_ref, k_ref, v_ref, halo_ref, key_ref, filt_ref, decay_ref, residue_ref,
    fwd_ref, inv_ref, taps_ref, near_ref, group_ref, out_ref, sum_ref,
):
    blocks = q_ref.shape[0] // LEN
    half = LEN // 2
    modes = decay_ref.shape[0]
    fwd_all = fwd_ref[...]
    fwd = fwd_all[: 2 * LEN]
    inv = inv_ref[...]
    decay = decay_ref[...]
    residue = residue_ref[...]
    width = decay.shape[1]
    node_col = column(nodes)

    def at_nodes(weights):
        total = None
        for m in range(modes):
            part = node_rows[m] * weights[m : m + 1]
            total = part if total is None else total + part
        return total

    node_rows = [jnp.exp(-node_col * decay[m : m + 1]) for m in range(modes)]
    mode_rows = [jnp.exp(-np.float32(node) * decay) for node in nodes]
    weight = residue * jnp.exp(-decay)
    step = jnp.exp(-np.float32(LEN) * decay)

    expanded = lax.dot_general(
        filt_ref[...], group_ref[...], (((0,), (0,)), ((), ())), preferred_element_type=F32
    ).astype(BF16)
    short = dot(fwd, twice(expanded))
    short_re, short_im = short[:LEN], short[LEN:]
    long = dot(taps_ref[...], tripled(at_nodes(residue)))
    long_re, long_im = long[:LEN], long[LEN:]

    before = dot(fwd, twice(halo_ref[...]))
    state = None
    for i in range(blocks):
        rows = pl.ds(i * LEN, LEN)
        product = (k_ref[rows, :].astype(F32) * v_ref[rows, :].astype(F32)).astype(BF16)
        now = dot(fwd, twice(product))
        turned_re = jnp.concatenate(
            [
                now[:half] - before[LEN : LEN + half],
                now[half:LEN] + before[LEN + half :],
            ],
            axis=0,
        )
        turned_im = jnp.concatenate(
            [
                now[LEN : LEN + half] + before[:half],
                now[LEN + half :] - before[half:LEN],
            ],
            axis=0,
        )
        convolved = dot(inv, times(turned_re, turned_im, short_re, short_im))
        before = now
        li_input = key_ref[rows, :].astype(F32) * (q_ref[rows, :].astype(F32) * convolved)
        seen = dot(fwd_all, twice(li_input.astype(BF16)))
        value = dot(inv, times(seen[:LEN], seen[LEN : 2 * LEN], long_re, long_im))
        if state is not None:
            value = value + dot(near_ref[...], tripled(at_nodes(weight * state)))
        out_ref[rows, :] = value
        ended = None
        for k in range(len(nodes)):
            part = mode_rows[k] * seen[2 * LEN + k : 2 * LEN + k + 1]
            ended = part if ended is None else ended + part
        state = ended if state is None else step * state + ended
    sum_ref[...] = state


def far_kernel(nodes, value_ref, query_ref, state_ref, decay_ref, residue_ref, far_ref, out_ref):
    decay = decay_ref[...]
    start = residue_ref[...] * state_ref[...]
    node_col = column(nodes + 1.0)
    total = None
    for m in range(decay.shape[0]):
        part = jnp.exp(-node_col * decay[m : m + 1]) * start[m : m + 1]
        total = part if total is None else total + part
    long_conv = value_ref[...] + dot(far_ref[...], tripled(total))
    out_ref[...] = (query_ref[...].astype(F32) * long_conv).astype(BF16)


def per_device(mr_qkv, mr_filter, li_gates, decay, residue):
    rows = mr_qkv.shape[0]
    channels = mr_qkv.shape[1] // 3
    modes = decay.shape[1]
    count, mine = lax.axis_size("ctx"), lax.axis_index("ctx")
    edge = (
        mr_qkv[rows - LEN :, channels : 2 * channels].astype(F32)
        * mr_qkv[rows - LEN :, 2 * channels :].astype(F32)
    ).astype(BF16)
    halo = lax.ppermute(edge, "ctx", [(i - 1, i) for i in range(1, count)])
    decay_rows = decay.T
    residue_rows = residue.T

    width = 256
    tiles = channels // width
    nodes, *consts = tables(width)
    consts = [jnp.asarray(c, BF16) for c in consts]
    whole = lambda c: pl.BlockSpec(c.shape, lambda j: (0, 0))
    part = lambda height, k: pl.BlockSpec((height, width), lambda j, k=k: (0, k * tiles + j))
    values, ended = pl.pallas_call(
        functools.partial(near_kernel, nodes),
        grid=(tiles,),
        in_specs=[
            part(rows, 0), part(rows, 1), part(rows, 2), part(LEN, 0), part(rows, 1),
            pl.BlockSpec((width // 16, LEN), lambda j: (j, 0)),
            part(modes, 0), part(modes, 0),
        ] + [whole(c) for c in consts],
        out_specs=[part(rows, 0), part(modes, 0)],
        out_shape=[
            jax.ShapeDtypeStruct((rows, channels), F32),
            jax.ShapeDtypeStruct((modes, channels), F32),
        ],
        compiler_params=pltpu.CompilerParams(vmem_limit_bytes=48 * 2**20),
        name="near",
    )(mr_qkv, mr_qkv, mr_qkv, halo, li_gates, mr_filter, decay_rows, residue_rows, *consts)

    share = channels // count
    mine_all = lax.all_to_all(
        ended.reshape(modes, count, share), "ctx", split_axis=1, concat_axis=0, tiled=False
    ).reshape(count, modes, share)
    own_decay = jnp.exp(-lax.dynamic_slice_in_dim(decay_rows, mine * share, share, 1) * rows)
    running = jnp.zeros_like(own_decay)
    starts = []
    for k in range(count):
        starts.append(running)
        running = own_decay * running + mine_all[k]
    incoming = lax.all_to_all(
        jnp.stack(starts), "ctx", split_axis=0, concat_axis=1, tiled=False
    ).reshape(modes, channels)

    far_nodes, far_basis = lagrange(rows, FAR_NODES)
    far_high, far_low = halves(far_basis)
    far = jnp.asarray(np.concatenate([far_high, far_low, far_high], axis=1), BF16)
    return pl.pallas_call(
        functools.partial(far_kernel, far_nodes),
        grid=(tiles,),
        in_specs=[
            part(rows, 0), part(rows, 0), part(modes, 0), part(modes, 0), part(modes, 0), whole(far)
        ],
        out_specs=part(rows, 0),
        out_shape=jax.ShapeDtypeStruct((rows, channels), BF16),
        compiler_params=pltpu.CompilerParams(vmem_limit_bytes=48 * 2**20),
        name="far",
    )(values, li_gates, incoming, decay_rows, residue_rows, far)


def solution(mesh):
    return jax.shard_map(
        per_device,
        mesh=mesh,
        in_specs=(P(("groups", "ctx"), None), P(), P(("groups", "ctx"), None), P(), P()),
        out_specs=P(("groups", "ctx"), None),
        check_vma=False,
    )
```

profile of v0, /device:TPU:1, one launch (start us, length us, event | category | flops | bytes accessed | tf_op | source)
XLA Modules:
  0.0 114.9 jit_solution(16168587762116912799)
XLA Ops:
  0.0 1.8 %multiply_convert_fusion = bf16[128,4096]{1,0:T(8,128)(2,1)S(1)} fusion(bf16[512,12288]{1,0:T(8,128)(2,1)} %v_ref.1), kind=kLoop, calls=%fused_computation | loop fusion | flops 2097152 | bytes 3145728 | tf_op jit(solution)/shard_map/convert_element_type | solution.py:178
  1.8 4.5 %collective-permute-start = (bf16[128,4096]{1,0:T(8,128)(2,1)S(1)}, bf16[128,4096]{1,0:T(8,128)(2,1)S(1)}, u32[]{:S(2)}, u32[]{:S(2)}) collective-permute-start(bf16[128,4096]{1,0:T(8,128)(2,1)S(1)} %multiply_convert_fusion), channel_id=1, source_target_pairs={{0,1},{1,2},{2,3},{3,4},{4,5},{5,6},{6,7},{7,8},{8,9},{9,10},{10,1... | collective-permute-start | bytes 3145736 | tf_op jit(solution)/shard_map/ppermute | solution.py:179
  6.3 11.7 %collective-permute-done.halo_ref = bf16[128,4096]{1,0:T(8,128)(2,1)S(1)} collective-permute-done((bf16[128,4096]{1,0:T(8,128)(2,1)S(1)}, bf16[128,4096]{1,0:T(8,128)(2,1)S(1)}, u32[]{:S(2)}, u32[]{:S(2)}) %collective-permute-start) | collective-permute-done | bytes 1048608 | tf_op jit(solution)/shard_map/ppermute | solution.py:179
  18.1 0.0 copy-start
  18.1 0.9 copy-done
  19.0 0.0 copy-start.2
  19.0 0.9 copy-done.2
  20.0 0.0 copy-start.4
  20.0 0.9 copy-done.4
  20.9 0.0 copy-start.6
  20.9 0.8 copy-done.6
  21.7 0.0 copy-start.7
  21.7 0.8 copy-done.7
  22.6 0.0 copy-start.8
  22.6 0.8 copy-done.8
  23.4 0.0 copy-start.9
  23.4 0.8 copy-done.9
  24.1 0.0 copy-start.10
  24.2 0.7 copy-done.10
  24.8 0.0 copy-start.1
  24.8 0.0 copy-start.3
  24.9 0.0 copy-start.5
  24.9 45.1 %near.1 = (f32[512,4096]{1,0:T(8,128)}, f32[16,4096]{1,0:T(8,128)S(1)}) custom-call(bf16[512,12288]{1,0:T(8,128)(2,1)} %v_ref.1, bf16[512,12288]{1,0:T(8,128)(2,1)} %v_ref.1, bf16[512,12288]{1,0:T(8,128)(2,1)} %v_ref.1, bf16[128,4096]{1,0:T(8,128)(2,1)S(1)} %collective-permute-done.halo_ref, bf16[512,8192]{1,0:T(8,128)(2,1)} %query_ref.1, ...), custom_call_target="tpu_custom_call" | custom-call | tf_op jit(solution)/shard_map/near/pallas_call | solution.py:189
  70.0 0.1 copy.31
  70.1 0.9 copy.14
  70.9 7.2 %all-to-all-start = ((f32[1,16,16,256]{3,1,0,2:T(8,128)}), f32[1,16,16,256]{3,1,0,2:T(8,128)S(1)}, u32[]{:S(2)}, u32[]{:S(2)}) async-start(f32[1,16,16,256]{3,1,0,2:T(8,128)} %copy.14), calls=%async_computation | async-start | bytes 524288 | tf_op jit(solution)/shard_map/all_to_all | solution.py:207
  78.1 9.5 %all-to-all-done = f32[1,16,16,256]{3,1,0,2:T(8,128)S(1)} async-done(((f32[1,16,16,256]{3,1,0,2:T(8,128)}), f32[1,16,16,256]{3,1,0,2:T(8,128)S(1)}, u32[]{:S(2)}, u32[]{:S(2)}) %all-to-all-start) | async-done | bytes 262176 | tf_op jit(solution)/shard_map/all_to_all | solution.py:207
  87.6 0.0 copy-done.1
  88.1 12.8 %all_to_all.30 = f32[16,16,1,256]{3,1,2,0:T(8,128)S(1)} all-to-all(f32[16,16,1,256]{3,1,2,0:T(8,128)S(1)} %bitcast.291), channel_id=1, replica_groups=mesh['groups'=2,'ctx'=16] {'ctx'}, dimensions={0} | all-to-all | bytes 524288 | tf_op jit(solution)/shard_map/all_to_all | solution.py:216
  100.9 0.0 copy-done.3
  100.9 0.0 copy-done.5
  100.9 13.9 %far.1 = bf16[512,4096]{1,0:T(8,128)(2,1)} custom-call(f32[512,4096]{1,0:T(8,128)} %get-tuple-element.7.value_ref, bf16[512,8192]{1,0:T(8,128)(2,1)} %query_ref.1, f32[16,4096]{1,0:T(8,128)S(1)} %bitcast.271, f32[16,4096]{1,0:T(8,128)S(1)} %bitcast.268, f32[16,4096]{1,0:T(8,128)S(1)} %bitcast.270, bf16[512,96]{1,0:T(8,128)(2,1)S(1)} %copy-done.5), custom_call_target="tpu_custom_call" | custom-call | tf_op jit(solution)/shard_map/far/pallas_call | solution.py:223
  (17 shorter events, 0.3 us)
Async XLA Ops:
  1.8 16.3 %collective-permute-start = (bf16[128,4096]{1,0:T(8,128)(2,1)S(1)}, bf16[128,4096]{1,0:T(8,128)(2,1)S(1)}, u32[]{:S(2)}, u32[]{:S(2)}) collective-permute-start(bf16[128,4096]{1,0:T(8,128)(2,1)S(1)} %multiply_convert_fusion), channel_id=1, source_target_pairs={{0,1},{1,2},{2,3},{3,4},{4,5},{5,6},{6,7},{7,8},{8,9},{9,10},{10,1... | collective-permute-start | bytes 3145736 | tf_op jit(solution)/shard_map/ppermute | solution.py:179
  18.1 0.9 copy-start
  19.0 0.9 copy-start.2
  20.0 0.9 copy-start.4
  20.9 0.8 copy-start.6
  21.7 0.8 copy-start.7
  22.6 0.8 copy-start.8
  23.4 0.8 copy-start.9
  24.1 0.7 copy-start.10
  24.8 62.8 %copy-start.1 = (f32[4096,16]{0,1:T(8,128)S(1)}, f32[4096,16]{0,1:T(8,128)}, u32[]{:S(2)}) copy-start(f32[4096,16]{0,1:T(8,128)} %param.14) | copy-start | bytes 786436
  24.8 76.1 %copy-start.3 = (f32[4096,16]{0,1:T(8,128)S(1)}, f32[4096,16]{0,1:T(8,128)}, u32[]{:S(2)}) copy-start(f32[4096,16]{0,1:T(8,128)} %param.15) | copy-start | bytes 786436
  24.9 76.1 %copy-start.5 = (bf16[512,96]{1,0:T(8,128)(2,1)S(1)}, bf16[512,96]{1,0:T(8,128)(2,1)}, u32[]{:S(2)}) copy-start(bf16[512,96]{1,0:T(8,128)(2,1)} %constant.32.clone.far_ref) | copy-start | bytes 294916
  70.9 16.7 %all-to-all-start = ((f32[1,16,16,256]{3,1,0,2:T(8,128)}), f32[1,16,16,256]{3,1,0,2:T(8,128)S(1)}, u32[]{:S(2)}, u32[]{:S(2)}) async-start(f32[1,16,16,256]{3,1,0,2:T(8,128)} %copy.14), calls=%async_computation | async-start | bytes 524288 | tf_op jit(solution)/shard_map/all_to_all | solution.py:207
where the time goes:
time: 116 us; the launch traced here: 115 us
  Pallas kernels  59.1 us (51%)
  waiting for transfers between devices  21.2 us (18%)
  blocking collectives  12.8 us (11%)
  starting transfers between devices  11.7 us (10%)
  local copies, waits for them, and re-layouts  7.75 us (7%)
  other arithmetic  2.1 us (2%)
    pallas_call x1, Pallas kernels, per_device(): pl.pallas_call(functools.partial(near_kernel, nodes), grid=(tiles,), in_s...  45.1 us
    pallas_call x1, Pallas kernels, per_device(): pl.pallas_call(functools.partial(far_kernel, far_nodes), grid=(tiles,), i...  13.9 us
    all_to_all x1, blocking collectives, per_device(): lax.all_to_all(jnp.stack(starts), 'ctx', split_axis=0, concat_axis=1, til...  12.8 us
    ppermute x1, waiting for transfers between devices, per_device(): halo = lax.ppermute(edge, 'ctx', [(i - 1, i) for i in range(1, count)])  11.7 us
    all_to_all x1, waiting for transfers between devices, per_device(): lax.all_to_all(ended.reshape(modes, count, share), 'ctx', split_axis=1, c...  9.49 us
    all_to_all x1, starting transfers between devices, per_device(): lax.all_to_all(ended.reshape(modes, count, share), 'ctx', split_axis=1, c...  7.2 us
    unnamed x25, local copies, waits for them, and re-layouts  6.89 us
    ppermute x1, starting transfers between devices, per_device(): halo = lax.ppermute(edge, 'ctx', [(i - 1, i) for i in range(1, count)])  4.54 us
  transfers between devices with their start and end apart: 2, of which 2 were waited for; matrix products, arithmetic and copies ran while one was open for 0% of the time, Pallas kernels for 0%

commit v1 on v0

--- a/solution.py
+++ b/solution.py
@@ -49,7 +49,19 @@
     near_high, near_low = halves(basis)
     near = np.concatenate([near_high, near_low, near_high], axis=1)
     group = np.arange(width)[None, :] // 16 == np.arange(width // 16)[:, None]
-    return nodes, fwd, inverse, taps, near, group
+    packed, spans, start = [], [], 0
+    for table in (fwd, inverse, near, taps, group):
+        table = np.asarray(table, BF16)
+        height, depth = table.shape
+        spans.append((start, start + height, depth))
+        packed.append(np.pad(table, ((0, 0), (0, 2 * LEN - depth))))
+        start += height
+    return nodes, np.concatenate(packed, axis=0), spans
+
+
+def table_at(packed_ref, span):
+    first, last, depth = span
+    return packed_ref[first:last, :depth]
 
 
 def dot(a, b):
@@ -84,40 +96,54 @@
     return total
 
 
+def weighted(rows_ref, weights):
+    total = None
+    for m in range(weights.shape[0]):
+        part = rows_ref[m * NODES : (m + 1) * NODES, :] * weights[m : m + 1]
+        total = part if total is None else total + part
+    return total
+
+
+def prepare_kernel(
+    nodes, spans, filt_ref, decay_ref, residue_ref, packed_ref,
+    short_ref, long_ref, node_ref, mode_ref,
+):
+    fwd = table_at(packed_ref, spans[0])[: 2 * LEN]
+    decay = decay_ref[...]
+    modes = decay.shape[0]
+    node_col = column(nodes)
+    for m in range(modes):
+        node_ref[m * NODES : (m + 1) * NODES, :] = jnp.exp(-node_col * decay[m : m + 1])
+    for k, node in enumerate(nodes):
+        mode_ref[k * modes : (k + 1) * modes, :] = jnp.exp(-np.float32(node) * decay)
+    expanded = lax.dot_general(
+        filt_ref[...],
+        table_at(packed_ref, spans[4]),
+        (((0,), (0,)), ((), ())),
+        preferred_element_type=F32,
+    ).astype(BF16)
+    short_ref[...] = dot(fwd, twice(expanded))
+    long_ref[...] = dot(
+        table_at(packed_ref, spans[3]), tripled(weighted(node_ref, residue_ref[...]))
+    )
+
+
 def near_kernel(
-    nodes, q_ref, k_ref, v_ref, halo_ref, key_ref, filt_ref, decay_ref, residue_ref,
-    fwd_ref, inv_ref, taps_ref, near_ref, group_ref, out_ref, sum_ref,
+    spans, q_ref, k_ref, v_ref, halo_ref, key_ref, decay_ref, residue_ref,
+    short_ref, long_ref, node_ref, mode_ref, packed_ref, out_ref, sum_ref,
 ):
     blocks = q_ref.shape[0] // LEN
     half = LEN // 2
     modes = decay_ref.shape[0]
-    fwd_all = fwd_ref[...]
+    fwd_all = table_at(packed_ref, spans[0])
     fwd = fwd_all[: 2 * LEN]
-    inv = inv_ref[...]
+    inv = table_at(packed_ref, spans[1])
+    near = table_at(packed_ref, spans[2])
     decay = decay_ref[...]
-    residue = residue_ref[...]
-    width = decay.shape[1]
-    node_col = column(nodes)
-
-    def at_nodes(weights):
-        total = None
-        for m in range(modes):
-            part = node_rows[m] * weights[m : m + 1]
-            total = part if total is None else total + part
-        return total
-
-    node_rows = [jnp.exp(-node_col * decay[m : m + 1]) for m in range(modes)]
-    mode_rows = [jnp.exp(-np.float32(node) * decay) for node in nodes]
-    weight = residue * jnp.exp(-decay)
+    weight = residue_ref[...] * jnp.exp(-decay)
     step = jnp.exp(-np.float32(LEN) * decay)
-
-    expanded = lax.dot_general(
-        filt_ref[...], group_ref[...], (((0,), (0,)), ((), ())), preferred_element_type=F32
-    ).astype(BF16)
-    short = dot(fwd, twice(expanded))
-    short_re, short_im = short[:LEN], short[LEN:]
-    long = dot(taps_ref[...], tripled(at_nodes(residue)))
-    long_re, long_im = long[:LEN], long[LEN:]
+    short_re, short_im = short_ref[:LEN, :], short_ref[LEN:, :]
+    long_re, long_im = long_ref[:LEN, :], long_ref[LEN:, :]
 
     before = dot(fwd, twice(halo_ref[...]))
     state = None
@@ -145,14 +171,101 @@
         seen = dot(fwd_all, twice(li_input.astype(BF16)))
         value = dot(inv, times(seen[:LEN], seen[LEN : 2 * LEN], long_re, long_im))
         if state is not None:
-            value = value + dot(near_ref[...], tripled(at_nodes(weight * state)))
+            value = value + dot(near, tripled(weighted(node_ref, weight * state)))
         out_ref[rows, :] = value
         ended = None
-        for k in range(len(nodes)):
-            part = mode_rows[k] * seen[2 * LEN + k : 2 * LEN + k + 1]
+        for k in range(NODES):
+            part = mode_ref[k * modes : (k + 1) * modes, :] * seen[2 * LEN + k : 2 * LEN + k + 1]
             ended = part if ended is None else ended + part
         state = ended if state is None else step * state + ended
     sum_ref[...] = state
+
+
+def exchange_kernel(
+    count, tokens, ended_ref, decay_ref, out_ref, got, starts, landed,
+    send_one, recv_one, send_two, recv_two,
+):
+    mine = lax.axis_index("ctx")
+    share = got.shape[2]
+
+    def other(k):
+        return lax.rem(mine + k, count)
+
+    def columns(k):
+        return pl.ds(pl.multiple_of(k * share, share), share)
+
+    def first(k):
+        return pltpu.make_async_remote_copy(
+            src_ref=ended_ref.at[:, columns(k)],
+            dst_ref=got.at[mine],
+            send_sem=send_one.at[k],
+            recv_sem=recv_one.at[mine],
+            device_id={"ctx": k},
+            device_id_type=pl.DeviceIdType.MESH,
+        )
+
+    def arrived(buffer, sem, k):
+        return pltpu.make_async_remote_copy(
+            src_ref=buffer.at[k],
+            dst_ref=buffer.at[k],
+            send_sem=sem.at[k],
+            recv_sem=sem.at[k],
+            device_id={"ctx": k},
+            device_id_type=pl.DeviceIdType.MESH,
+        )
+
+    def second(k):
+        return pltpu.make_async_remote_copy(
+            src_ref=starts.at[k],
+            dst_ref=landed.at[mine],
+            send_sem=send_two.at[k],
+            recv_sem=recv_two.at[mine],
+            device_id={"ctx": k},
+            device_id_type=pl.DeviceIdType.MESH,
+        )
+
+    barrier = pltpu.get_barrier_semaphore()
+
+    @pl.loop(1, count)
+    def _(k):
+        pl.semaphore_signal(
+            barrier, inc=1, device_id={"ctx": other(k)}, device_id_type=pl.DeviceIdType.MESH
+        )
+
+    pl.semaphore_wait(barrier, count - 1)
+
+    @pl.loop(1, count)
+    def _(k):
+        first(other(k)).start()
+
+    got[mine] = ended_ref[:, columns(mine)]
+    own_decay = jnp.exp(-np.float32(tokens) * decay_ref[:, columns(mine)])
+
+    def turn(k, running):
+        starts[k] = running
+
+        @pl.when(k != mine)
+        def _():
+            second(k).start()
+            arrived(got, recv_one, k).wait_recv()
+
+        return own_decay * running + got[k]
+
+    lax.fori_loop(0, count, turn, jnp.zeros(own_decay.shape, F32))
+    landed[mine] = starts[mine]
+
+    @pl.loop(1, count)
+    def _(k):
+        arrived(landed, recv_two, other(k)).wait_recv()
+
+    @pl.loop(0, count)
+    def _(k):
+        out_ref[:, columns(k)] = landed[k]
+
+    @pl.loop(1, count)
+    def _(k):
+        first(other(k)).wait_send()
+        second(other(k)).wait_send()
 
 
 def far_kernel(nodes, value_ref, query_ref, state_ref, decay_ref, residue_ref, far_ref, out_ref):
@@ -171,7 +284,7 @@
     rows = mr_qkv.shape[0]
     channels = mr_qkv.shape[1] // 3
     modes = decay.shape[1]
-    count, mine = lax.axis_size("ctx"), lax.axis_index("ctx")
+    count = lax.axis_size("ctx")
     edge = (
         mr_qkv[rows - LEN :, channels : 2 * channels].astype(F32)
         * mr_qkv[rows - LEN :, 2 * channels :].astype(F32)
@@ -182,40 +295,49 @@
 
     width = 256
     tiles = channels // width
-    nodes, *consts = tables(width)
-    consts = [jnp.asarray(c, BF16) for c in consts]
+    nodes, packed, spans = tables(width)
+    packed = jnp.asarray(packed)
     whole = lambda c: pl.BlockSpec(c.shape, lambda j: (0, 0))
-    part = lambda height, k: pl.BlockSpec((height, width), lambda j, k=k: (0, k * tiles + j))
-    values, ended = pl.pallas_call(
-        functools.partial(near_kernel, nodes),
+    part = lambda height, k=0: pl.BlockSpec((height, width), lambda j, k=k: (0, k * tiles + j))
+    shape = lambda height: jax.ShapeDtypeStruct((height, channels), F32)
+    params = pltpu.CompilerParams(vmem_limit_bytes=48 * 2**20)
+    heights = (2 * LEN, 2 * LEN, modes * NODES, modes * NODES)
+    prepared = pl.pallas_call(
+        functools.partial(prepare_kernel, nodes, spans),
         grid=(tiles,),
         in_specs=[
-            part(rows, 0), part(rows, 1), part(rows, 2), part(LEN, 0), part(rows, 1),
             pl.BlockSpec((width // 16, LEN), lambda j: (j, 0)),
-            part(modes, 0), part(modes, 0),
-        ] + [whole(c) for c in consts],
-        out_specs=[part(rows, 0), part(modes, 0)],
-        out_shape=[
-            jax.ShapeDtypeStruct((rows, channels), F32),
-            jax.ShapeDtypeStruct((modes, channels), F32),
+            part(modes), part(modes), whole(packed),
         ],
-        compiler_params=pltpu.CompilerParams(vmem_limit_bytes=48 * 2**20),
+        out_specs=[part(height) for height in heights],
+        out_shape=[shape(height) for height in heights],
+        compiler_params=params,
+        name="prepare",
+    )(mr_filter, decay_rows, residue_rows, packed)
+    values, ended = pl.pallas_call(
+        functools.partial(near_kernel, spans),
+        grid=(tiles,),
+        in_specs=[
+            part(rows, 0), part(rows, 1), part(rows, 2), part(LEN), part(rows, 1),
+            part(modes), part(modes),
+        ] + [part(height) for height in heights] + [whole(packed)],
+        out_specs=[part(rows), part(modes)],
+        out_shape=[shape(rows), shape(modes)],
+        compiler_params=params,
         name="near",
-    )(mr_qkv, mr_qkv, mr_qkv, halo, li_gates, mr_filter, decay_rows, residue_rows, *consts)
+    )(mr_qkv, mr_qkv, mr_qkv, halo, li_gates, decay_rows, residue_rows, *prepared, packed)
 
     share = channels // count
-    mine_all = lax.all_to_all(
-        ended.reshape(modes, count, share), "ctx", split_axis=1, concat_axis=0, tiled=False
-    ).reshape(count, modes, share)
-    own_decay = jnp.exp(-lax.dynamic_slice_in_dim(decay_rows, mine * share, share, 1) * rows)
-    running = jnp.zeros_like(own_decay)
-    starts = []
-    for k in range(count):
-        starts.append(running)
-        running = own_decay * running + mine_all[k]
-    incoming = lax.all_to_all(
-        jnp.stack(starts), "ctx", split_axis=0, concat_axis=1, tiled=False
-    ).reshape(modes, channels)
+    slots = pltpu.VMEM((count, modes, share), F32)
+    incoming = pl.pallas_call(
+        functools.partial(exchange_kernel, count, rows),
+        in_specs=[pl.BlockSpec(memory_space=pltpu.VMEM)] * 2,
+        out_specs=pl.BlockSpec(memory_space=pltpu.VMEM),
+        out_shape=shape(modes),
+        scratch_shapes=[slots] * 3 + [pltpu.SemaphoreType.DMA((count,))] * 4,
+        compiler_params=pltpu.CompilerParams(collective_id=0, has_side_effects=True),
+        name="exchange",
+    )(ended, decay_rows)
 
     far_nodes, far_basis = lagrange(rows, FAR_NODES)
     far_high, far_low = halves(far_basis)
@@ -224,9 +346,9 @@
         functools.partial(far_kernel, far_nodes),
         grid=(tiles,),
         in_specs=[
-            part(rows, 0), part(rows, 0), part(modes, 0), part(modes, 0), part(modes, 0), whole(far)
+            part(rows), part(rows), part(modes), part(modes), part(modes), whole(far)
         ],
-        out_specs=part(rows, 0),
+        out_specs=part(rows),
         out_shape=jax.ShapeDtypeStruct((rows, channels), BF16),
         compiler_params=pltpu.CompilerParams(vmem_limit_bytes=48 * 2**20),
         name="far",

time: 116 us -> 97.9 us (0.84)
  Pallas kernels: 59.1 us -> 82.7 us
  waiting for transfers between devices: 21.2 us -> 0.01 us
  blocking collectives: 12.8 us -> 0 us
  starting transfers between devices: 11.7 us -> 4.54 us
    pallas_call x1 -> x3, Pallas kernels: 45.1 us -> 68.8 us  [the longest x1 40.4 us: per_device(): pl.pallas_call(functools.partial(near_kernel, spans), grid=(tiles,), in_s...]
    all_to_all x1 -> x0, blocking collectives: 12.8 us -> none  [per_device(): lax.all_to_all(jnp.stack(starts), 'ctx', split_axis=0, concat_axis=1, til...]
    ppermute x1, waiting for transfers between devices: 11.7 us -> 0.01 us  [per_device(): halo = lax.ppermute(edge, 'ctx', [(i - 1, i) for i in range(1, count)])]
    all_to_all x1 -> x0, waiting for transfers between devices: 9.49 us -> none  [per_device(): lax.all_to_all(ended.reshape(modes, count, share), 'ctx', split_axis=1, c...]
    all_to_all x1 -> x0, starting transfers between devices: 7.2 us -> none  [per_device(): lax.all_to_all(ended.reshape(modes, count, share), 'ctx', split_axis=1, c...]
    unnamed x25 -> x24, local copies, waits for them, and re-layouts: 6.89 us -> 7.35 us
  transfers between devices with their start and end apart: 2 -> 1, of which waited for: 2 -> 0; matrix products, arithmetic and copies ran while one was open for 0% -> 0% of each run, Pallas kernels for 0% -> 11%
where the time goes in v1:
time: 97.9 us; the launch traced here: 96.6 us
  Pallas kernels  82.7 us (84%)
  local copies, waits for them, and re-layouts  7.35 us (8%)
  starting transfers between devices  4.54 us (5%)
  other arithmetic  1.87 us (2%)
    pallas_call x1, Pallas kernels, per_device(): pl.pallas_call(functools.partial(near_kernel, spans), grid=(tiles,), in_s...  40.4 us
    pallas_call x1, Pallas kernels, per_device(): pl.pallas_call(functools.partial(exchange_kernel, count, rows), in_specs=...  17.4 us
    pallas_call x1, Pallas kernels, per_device(): pl.pallas_call(functools.partial(far_kernel, far_nodes), grid=(tiles,), i...  13.9 us
    pallas_call x1, Pallas kernels, per_device(): pl.pallas_call(functools.partial(prepare_kernel, nodes, spans), grid=(til...  11.1 us
    unnamed x24, local copies, waits for them, and re-layouts  7.35 us
    ppermute x1, starting transfers between devices, per_device(): halo = lax.ppermute(edge, 'ctx', [(i - 1, i) for i in range(1, count)])  4.54 us
  transfers between devices with their start and end apart: 1, of which 0 were waited for; matrix products, arithmetic and copies ran while one was open for 0% of the time, Pallas kernels for 11%

profile of v1, /device:TPU:1, one launch (start us, length us, event | category | flops | bytes accessed | tf_op | source)
XLA Modules:
  0.0 96.6 jit_solution(6584967602353849624)
XLA Ops:
  0.0 0.0 copy-start.7
  0.0 0.0 copy-start.5
  0.0 0.0 copy-start.1
  0.0 1.9 %multiply_convert_fusion = bf16[128,4096]{1,0:T(8,128)(2,1)S(1)} fusion(bf16[512,12288]{1,0:T(8,128)(2,1)} %v_ref.1), kind=kLoop, calls=%fused_computation | loop fusion | flops 2097152 | bytes 3145728 | tf_op jit(solution)/shard_map/convert_element_type | solution.py:291
  1.9 4.5 %collective-permute-start = (bf16[128,4096]{1,0:T(8,128)(2,1)S(1)}, bf16[128,4096]{1,0:T(8,128)(2,1)S(1)}, u32[]{:S(2)}, u32[]{:S(2)}) collective-permute-start(bf16[128,4096]{1,0:T(8,128)(2,1)S(1)} %multiply_convert_fusion), channel_id=1, source_target_pairs={{0,1},{1,2},{2,3},{3,4},{4,5},{5,6},{6,7},{7,8},{8,9},{9,10},{10,1... | collective-permute-start | bytes 3145736 | tf_op jit(solution)/shard_map/ppermute | solution.py:292
  6.4 0.0 copy-start
  6.4 0.9 copy-done
  7.4 0.0 copy-start.4
  7.4 0.9 copy-done.4
  8.3 0.0 copy-start.6
  8.3 1.0 %copy-done.6 = bf16[800,256]{1,0:T(8,128)(2,1)S(1)} copy-done((bf16[800,256]{1,0:T(8,128)(2,1)S(1)}, bf16[800,256]{1,0:T(8,128)(2,1)}, u32[]{:S(2)}) %copy-start.6) | copy-done | bytes 409624
  9.3 0.0 copy-start.11
  9.3 0.8 copy-done.11
  10.2 11.1 %prepare.1 = (f32[256,4096]{1,0:T(8,128)S(1)}, f32[256,4096]{1,0:T(8,128)}, f32[256,4096]{1,0:T(8,128)}, f32[256,4096]{1,0:T(8,128)}) custom-call(bf16[256,128]{1,0:T(8,128)(2,1)S(1)} %copy-done.11, f32[16,4096]{1,0:T(8,128)S(1)} %bitcast.3, f32[16,4096]{1,0:T(8,128)S(1)} %bitcast.6, bf16[800,256]{1,0:T(8,128)(2,1)S(1)} %copy-done.6), custom_call_target="tpu_custom_call" | custom-call | tf_op jit(solution)/shard_map/prepare/pallas_call | solution.py:305
  21.2 0.0 copy-start.3
  21.2 1.9 %copy-done.3 = f32[256,4096]{1,0:T(8,128)} copy-done((f32[256,4096]{1,0:T(8,128)}, f32[256,4096]{1,0:T(8,128)S(1)}, u32[]{:S(2)}) %copy-start.3) | copy-done | bytes 4194328
  23.2 0.0 collective-permute-done.halo_ref
  23.2 0.0 copy-done.7
  23.2 0.0 copy-done.5
  23.2 0.0 copy-done.1
  23.2 0.0 copy-start.2
  23.2 0.0 copy-start.10
  23.2 40.4 %near.1 = (f32[512,4096]{1,0:T(8,128)}, f32[16,4096]{1,0:T(8,128)S(1)}) custom-call(bf16[512,12288]{1,0:T(8,128)(2,1)} %v_ref.1, bf16[512,12288]{1,0:T(8,128)(2,1)} %v_ref.1, bf16[512,12288]{1,0:T(8,128)(2,1)} %v_ref.1, bf16[128,4096]{1,0:T(8,128)(2,1)S(1)} %collective-permute-done.halo_ref, bf16[512,8192]{1,0:T(8,128)(2,1)} %query_ref.1, ...), custom_call_target="tpu_custom_call" | custom-call | tf_op jit(solution)/shard_map/near/pallas_call | solution.py:317
  63.6 0.0 copy-start.9
  63.6 0.7 copy-done.9
  64.3 17.4 %exchange.1.state_ref = f32[16,4096]{1,0:T(8,128)} custom-call(f32[16,4096]{1,0:T(8,128)} %copy-done.9, f32[16,4096]{1,0:T(8,128)} %bitcast.2), custom_call_target="tpu_custom_call" | custom-call | tf_op jit(solution)/shard_map/exchange/pallas_call | solution.py:332
  81.7 0.0 copy-done.2
  81.7 0.0 copy-done.10
  81.7 0.0 copy-start.8
  81.7 0.9 copy-done.8
  82.7 13.9 %far.1 = bf16[512,4096]{1,0:T(8,128)(2,1)} custom-call(f32[512,4096]{1,0:T(8,128)} %get-tuple-element.15.value_ref, bf16[512,8192]{1,0:T(8,128)(2,1)} %query_ref.1, f32[16,4096]{1,0:T(8,128)S(1)} %copy-done.8, f32[16,4096]{1,0:T(8,128)S(1)} %bitcast.5, f32[16,4096]{1,0:T(8,128)S(1)} %bitcast.8, bf16[512,96]{1,0:T(8,128)(2,1)S(1)} %copy-done.10), custom_call_target="tpu_custom_call" | custom-call | tf_op jit(solution)/shard_map/far/pallas_call | solution.py:345
Async XLA Ops:
  0.0 23.2 %copy-start.7 = (bf16[800,256]{1,0:T(8,128)(2,1)S(1)}, bf16[800,256]{1,0:T(8,128)(2,1)}, u32[]{:S(2)}) copy-start(bf16[800,256]{1,0:T(8,128)(2,1)} %constant.4.clone.packed_ref) | copy-start | bytes 1228804
  0.0 23.2 %copy-start.5 = (f32[4096,16]{0,1:T(8,128)S(1)}, f32[4096,16]{0,1:T(8,128)}, u32[]{:S(2)}) copy-start(f32[4096,16]{0,1:T(8,128)} %param.11) | copy-start | bytes 786436
  0.0 23.2 %copy-start.1 = (f32[4096,16]{0,1:T(8,128)S(1)}, f32[4096,16]{0,1:T(8,128)}, u32[]{:S(2)}) copy-start(f32[4096,16]{0,1:T(8,128)} %param.10) | copy-start | bytes 786436
  1.9 21.3 %collective-permute-start = (bf16[128,4096]{1,0:T(8,128)(2,1)S(1)}, bf16[128,4096]{1,0:T(8,128)(2,1)S(1)}, u32[]{:S(2)}, u32[]{:S(2)}) collective-permute-start(bf16[128,4096]{1,0:T(8,128)(2,1)S(1)} %multiply_convert_fusion), channel_id=1, source_target_pairs={{0,1},{1,2},{2,3},{3,4},{4,5},{5,6},{6,7},{7,8},{8,9},{9,10},{10,1... | collective-permute-start | bytes 3145736 | tf_op jit(solution)/shard_map/ppermute | solution.py:292
  6.4 1.0 copy-start
  7.4 0.9 copy-start.4
  8.3 1.0 %copy-start.6 = (bf16[800,256]{1,0:T(8,128)(2,1)S(1)}, bf16[800,256]{1,0:T(8,128)(2,1)}, u32[]{:S(2)}) copy-start(bf16[800,256]{1,0:T(8,128)(2,1)} %constant.4.clone.packed_ref) | copy-start | bytes 1228804
  9.3 0.8 copy-start.11
  21.2 1.9 %copy-start.3 = (f32[256,4096]{1,0:T(8,128)}, f32[256,4096]{1,0:T(8,128)S(1)}, u32[]{:S(2)}) copy-start(f32[256,4096]{1,0:T(8,128)S(1)} %get-tuple-element.11.short_ref) | copy-start | bytes 12582916
  23.2 58.5 %copy-start.2 = (f32[4096,16]{0,1:T(8,128)S(1)}, f32[4096,16]{0,1:T(8,128)}, u32[]{:S(2)}) copy-start(f32[4096,16]{0,1:T(8,128)} %param.10) | copy-start | bytes 786436
  23.2 58.5 %copy-start.10 = (bf16[512,96]{1,0:T(8,128)(2,1)S(1)}, bf16[512,96]{1,0:T(8,128)(2,1)}, u32[]{:S(2)}) copy-start(bf16[512,96]{1,0:T(8,128)(2,1)} %constant.5.clone.far_ref) | copy-start | bytes 294916
  63.6 0.7 copy-start.9
  81.7 1.0 copy-start.8

commit v2 on v1

--- a/solution.py
+++ b/solution.py
@@ -12,7 +12,7 @@
 BF16 = jnp.bfloat16
 LEN = 128
 NODES = 16
-FAR_NODES = 32
+CHUNK = 256
 
 
 def halves(table):
@@ -96,61 +96,69 @@
     return total
 
 
-def weighted(rows_ref, weights):
+def weighted(rows_ref, base, weights):
     total = None
     for m in range(weights.shape[0]):
-        part = rows_ref[m * NODES : (m + 1) * NODES, :] * weights[m : m + 1]
+        first = base + m * NODES
+        part = rows_ref[first : first + NODES, :] * weights[m : m + 1]
         total = part if total is None else total + part
     return total
 
 
-def prepare_kernel(
-    nodes, spans, filt_ref, decay_ref, residue_ref, packed_ref,
-    short_ref, long_ref, node_ref, mode_ref,
-):
+def prepare_kernel(nodes, spans, filt_ref, modal_ref, packed_ref, out_ref):
     fwd = table_at(packed_ref, spans[0])[: 2 * LEN]
-    decay = decay_ref[...]
-    modes = decay.shape[0]
+    modes = modal_ref.shape[0] // 2
+    decay = modal_ref[:modes, :]
+    residue = modal_ref[modes:, :]
     node_col = column(nodes)
+    base = 4 * LEN
+    end = base + modes * NODES
     for m in range(modes):
-        node_ref[m * NODES : (m + 1) * NODES, :] = jnp.exp(-node_col * decay[m : m + 1])
+        out_ref[base + m * NODES : base + (m + 1) * NODES, :] = jnp.exp(-node_col * decay[m : m + 1])
     for k, node in enumerate(nodes):
-        mode_ref[k * modes : (k + 1) * modes, :] = jnp.exp(-np.float32(node) * decay)
-    expanded = lax.dot_general(
-        filt_ref[...],
-        table_at(packed_ref, spans[4]),
-        (((0,), (0,)), ((), ())),
-        preferred_element_type=F32,
-    ).astype(BF16)
-    short_ref[...] = dot(fwd, twice(expanded))
-    long_ref[...] = dot(
-        table_at(packed_ref, spans[3]), tripled(weighted(node_ref, residue_ref[...]))
-    )
-
-
-def near_kernel(
-    spans, q_ref, k_ref, v_ref, halo_ref, key_ref, decay_ref, residue_ref,
-    short_ref, long_ref, node_ref, mode_ref, packed_ref, out_ref, sum_ref,
+        out_ref[end + k * modes : end + (k + 1) * modes, :] = jnp.exp(-np.float32(node) * decay)
+    filters = CHUNK // 16
+    expanded = jnp.concatenate(
+        [
+            lax.dot_general(
+                filt_ref[i * filters : (i + 1) * filters, :],
+                table_at(packed_ref, spans[4]),
+                (((0,), (0,)), ((), ())),
+                preferred_element_type=F32,
+            ).astype(BF16)
+            for i in range(decay.shape[1] // CHUNK)
+        ],
+        axis=1,
+    )
+    out_ref[: 2 * LEN, :] = dot(fwd, twice(expanded))
+    out_ref[2 * LEN : 4 * LEN, :] = dot(
+        table_at(packed_ref, spans[3]), tripled(weighted(out_ref, base, residue))
+    )
+
+
+def near_chunk(
+    spans, q_ref, k_ref, v_ref, halo_ref, key_ref, modal_ref, prepared_ref, packed_ref,
+    out_ref, sum_ref,
 ):
     blocks = q_ref.shape[0] // LEN
     half = LEN // 2
-    modes = decay_ref.shape[0]
+    modes = modal_ref.shape[0] // 2
     fwd_all = table_at(packed_ref, spans[0])
     fwd = fwd_all[: 2 * LEN]
     inv = table_at(packed_ref, spans[1])
     near = table_at(packed_ref, spans[2])
-    decay = decay_ref[...]
-    weight = residue_ref[...] * jnp.exp(-decay)
+    base = 4 * LEN
+    end = base + modes * NODES
+    decay = modal_ref[:modes, :]
+    weight = modal_ref[modes:, :] * jnp.exp(-decay)
     step = jnp.exp(-np.float32(LEN) * decay)
-    short_re, short_im = short_ref[:LEN, :], short_ref[LEN:, :]
-    long_re, long_im = long_ref[:LEN, :], long_ref[LEN:, :]
-
-    before = dot(fwd, twice(halo_ref[...]))
-    state = None
+    spectra = [dot(fwd, twice(halo_ref[...]))]
     for i in range(blocks):
         rows = pl.ds(i * LEN, LEN)
         product = (k_ref[rows, :].astype(F32) * v_ref[rows, :].astype(F32)).astype(BF16)
-        now = dot(fwd, twice(product))
+        spectra.append(dot(fwd, twice(product)))
+    convolved = []
+    for before, now in zip(spectra[:-1], spectra[1:]):
         turned_re = jnp.concatenate(
             [
                 now[:half] - before[LEN : LEN + half],
@@ -165,20 +173,51 @@
             ],
             axis=0,
         )
-        convolved = dot(inv, times(turned_re, turned_im, short_re, short_im))
-        before = now
-        li_input = key_ref[rows, :].astype(F32) * (q_ref[rows, :].astype(F32) * convolved)
-        seen = dot(fwd_all, twice(li_input.astype(BF16)))
-        value = dot(inv, times(seen[:LEN], seen[LEN : 2 * LEN], long_re, long_im))
+        short_re, short_im = prepared_ref[:LEN, :], prepared_ref[LEN : 2 * LEN, :]
+        convolved.append(dot(inv, times(turned_re, turned_im, short_re, short_im)))
+    seen = []
+    for i in range(blocks):
+        rows = pl.ds(i * LEN, LEN)
+        li_input = key_ref[rows, :].astype(F32) * (q_ref[rows, :].astype(F32) * convolved[i])
+        seen.append(dot(fwd_all, twice(li_input.astype(BF16))))
+    state = None
+    for i in range(blocks):
+        rows = pl.ds(i * LEN, LEN)
+        long_re = prepared_ref[2 * LEN : 3 * LEN, :]
+        long_im = prepared_ref[3 * LEN : 4 * LEN, :]
+        value = dot(inv, times(seen[i][:LEN], seen[i][LEN : 2 * LEN], long_re, long_im))
         if state is not None:
-            value = value + dot(near, tripled(weighted(node_ref, weight * state)))
+            value = value + dot(near, tripled(weighted(prepared_ref, base, weight * state)))
         out_ref[rows, :] = value
         ended = None
         for k in range(NODES):
-            part = mode_ref[k * modes : (k + 1) * modes, :] * seen[2 * LEN + k : 2 * LEN + k + 1]
+            first = end + k * modes
+            weights = prepared_ref[first : first + modes, :]
+            part = weights * seen[i][2 * LEN + k : 2 * LEN + k + 1]
             ended = part if ended is None else ended + part
         state = ended if state is None else step * state + ended
     sum_ref[...] = state
+
+
+def near_kernel(spans, *refs):
+    packed_ref = refs[7]
+    for i in range(refs[0].shape[1] // CHUNK):
+        cut = lambda ref: ref.at[:, i * CHUNK : (i + 1) * CHUNK]
+        parts = [ref if ref is packed_ref else cut(ref) for ref in refs]
+        near_chunk(spans, *parts)
+
+
+def far_kernel(spans, value_ref, query_ref, state_ref, modal_ref, node_ref, packed_ref, out_ref):
+    modes = modal_ref.shape[0] // 2
+    decay = modal_ref[:modes, :]
+    near = table_at(packed_ref, spans[2])
+    step = jnp.exp(-np.float32(LEN) * decay)
+    start = modal_ref[modes:, :] * jnp.exp(-decay) * state_ref[...]
+    for i in range(value_ref.shape[0] // LEN):
+        rows = pl.ds(i * LEN, LEN)
+        long_conv = value_ref[rows, :] + dot(near, tripled(weighted(node_ref, 0, start)))
+        out_ref[rows, :] = (query_ref[rows, :].astype(F32) * long_conv).astype(BF16)
+        start = step * start
 
 
 def exchange_kernel(
@@ -239,7 +278,7 @@
         first(other(k)).start()
 
     got[mine] = ended_ref[:, columns(mine)]
-    own_decay = jnp.exp(-np.float32(tokens) * decay_ref[:, columns(mine)])
+    own_decay = jnp.exp(-np.float32(tokens) * decay_ref[: got.shape[1], columns(mine)])
 
     def turn(k, running):
         starts[k] = running
@@ -266,18 +305,6 @@
     def _(k):
         first(other(k)).wait_send()
         second(other(k)).wait_send()
-
-
-def far_kernel(nodes, value_ref, query_ref, state_ref, decay_ref, residue_ref, far_ref, out_ref):
-    decay = decay_ref[...]
-    start = residue_ref[...] * state_ref[...]
-    node_col = column(nodes + 1.0)
-    total = None
-    for m in range(decay.shape[0]):
-        part = jnp.exp(-node_col * decay[m : m + 1]) * start[m : m + 1]
-        total = part if total is None else total + part
-    long_conv = value_ref[...] + dot(far_ref[...], tripled(total))
-    out_ref[...] = (query_ref[...].astype(F32) * long_conv).astype(BF16)
 
 
 def per_device(mr_qkv, mr_filter, li_gates, decay, residue):
@@ -290,42 +317,40 @@
         * mr_qkv[rows - LEN :, 2 * channels :].astype(F32)
     ).astype(BF16)
     halo = lax.ppermute(edge, "ctx", [(i - 1, i) for i in range(1, count)])
-    decay_rows = decay.T
-    residue_rows = residue.T
-
-    width = 256
+    modal = jnp.concatenate([decay.T, residue.T], axis=0)
+
+    width = 512
     tiles = channels // width
-    nodes, packed, spans = tables(width)
+    nodes, packed, spans = tables(CHUNK)
     packed = jnp.asarray(packed)
     whole = lambda c: pl.BlockSpec(c.shape, lambda j: (0, 0))
     part = lambda height, k=0: pl.BlockSpec((height, width), lambda j, k=k: (0, k * tiles + j))
     shape = lambda height: jax.ShapeDtypeStruct((height, channels), F32)
     params = pltpu.CompilerParams(vmem_limit_bytes=48 * 2**20)
-    heights = (2 * LEN, 2 * LEN, modes * NODES, modes * NODES)
+    height = 4 * LEN + 2 * modes * NODES
     prepared = pl.pallas_call(
         functools.partial(prepare_kernel, nodes, spans),
         grid=(tiles,),
         in_specs=[
-            pl.BlockSpec((width // 16, LEN), lambda j: (j, 0)),
-            part(modes), part(modes), whole(packed),
-        ],
-        out_specs=[part(height) for height in heights],
-        out_shape=[shape(height) for height in heights],
+            pl.BlockSpec((width // 16, LEN), lambda j: (j, 0)), part(2 * modes), whole(packed)
+        ],
+        out_specs=part(height),
+        out_shape=shape(height),
         compiler_params=params,
         name="prepare",
-    )(mr_filter, decay_rows, residue_rows, packed)
+    )(mr_filter, modal, packed)
     values, ended = pl.pallas_call(
         functools.partial(near_kernel, spans),
         grid=(tiles,),
         in_specs=[
             part(rows, 0), part(rows, 1), part(rows, 2), part(LEN), part(rows, 1),
-            part(modes), part(modes),
-        ] + [part(height) for height in heights] + [whole(packed)],
+            part(2 * modes), part(height), whole(packed),
+        ],
         out_specs=[part(rows), part(modes)],
         out_shape=[shape(rows), shape(modes)],
         compiler_params=params,
         name="near",
-    )(mr_qkv, mr_qkv, mr_qkv, halo, li_gates, decay_rows, residue_rows, *prepared, packed)
+    )(mr_qkv, mr_qkv, mr_qkv, halo, li_gates, modal, prepared, packed)
 
     share = channels // count
     slots = pltpu.VMEM((count, modes, share), F32)
@@ -337,22 +362,22 @@
         scratch_shapes=[slots] * 3 + [pltpu.SemaphoreType.DMA((count,))] * 4,
         compiler_params=pltpu.CompilerParams(collective_id=0, has_side_effects=True),
         name="exchange",
-    )(ended, decay_rows)
-
-    far_nodes, far_basis = lagrange(rows, FAR_NODES)
-    far_high, far_low = halves(far_basis)
-    far = jnp.asarray(np.concatenate([far_high, far_low, far_high], axis=1), BF16)
+    )(ended, modal)
+
+    node_part = pl.BlockSpec(
+        (modes * NODES, width), lambda j: (4 * LEN // (modes * NODES), j)
+    )
     return pl.pallas_call(
-        functools.partial(far_kernel, far_nodes),
+        functools.partial(far_kernel, spans),
         grid=(tiles,),
         in_specs=[
-            part(rows), part(rows), part(modes), part(modes), part(modes), whole(far)
+            part(rows), part(rows), part(modes), part(2 * modes), node_part, whole(packed)
         ],
         out_specs=part(rows),
         out_shape=jax.ShapeDtypeStruct((rows, channels), BF16),
-        compiler_params=pltpu.CompilerParams(vmem_limit_bytes=48 * 2**20),
+        compiler_params=params,
         name="far",
-    )(values, li_gates, incoming, decay_rows, residue_rows, far)
+    )(values, li_gates, incoming, modal, prepared, packed)
 
 
 def solution(mesh):

time: 97.9 us -> 74.6 us (0.76)
  Pallas kernels: 82.7 us -> 61.6 us
  local copies, waits for them, and re-layouts: 7.35 us -> 4.55 us
  other arithmetic: 1.87 us -> 2.85 us
    pallas_call x1, Pallas kernels: 40.4 us -> 23.1 us  [per_device(): pl.pallas_call(functools.partial(near_kernel, spans), grid=(tiles,), in_s...]
    pallas_call x1, Pallas kernels: 13.9 us -> 10.5 us  [per_device(): pl.pallas_call(functools.partial(far_kernel, spans), grid=(tiles,), in_sp...]
    unnamed x24 -> x14, local copies, waits for them, and re-layouts: 7.35 us -> 4.55 us
    pallas_call x1, Pallas kernels: 11.1 us -> 8.3 us  [per_device(): pl.pallas_call(functools.partial(prepare_kernel, nodes, spans), grid=(til...]
    pallas_call x1, Pallas kernels: 17.4 us -> 19.7 us  [per_device(): pl.pallas_call(functools.partial(exchange_kernel, count, rows), in_specs=...]
    concatenate x0 -> x1, other arithmetic: none -> 1.07 us  [per_device(): modal = jnp.concatenate([decay.T, residue.T], axis=0)]
  transfers between devices with their start and end apart: 1 -> 1, of which waited for: 0 -> 1; matrix products, arithmetic and copies ran while one was open for 0% -> 1% of each run, Pallas kernels for 11% -> 11%
where the time goes in v2:
time: 74.6 us; the launch traced here: 74.1 us
  Pallas kernels  61.6 us (83%)
  local copies, waits for them, and re-layouts  4.55 us (6%)
  starting transfers between devices  4.54 us (6%)
  other arithmetic  2.85 us (4%)
    pallas_call x1, Pallas kernels, per_device(): pl.pallas_call(functools.partial(near_kernel, spans), grid=(tiles,), in_s...  23.1 us
    pallas_call x1, Pallas kernels, per_device(): pl.pallas_call(functools.partial(exchange_kernel, count, rows), in_specs=...  19.7 us
    pallas_call x1, Pallas kernels, per_device(): pl.pallas_call(functools.partial(far_kernel, spans), grid=(tiles,), in_sp...  10.5 us
    pallas_call x1, Pallas kernels, per_device(): pl.pallas_call(functools.partial(prepare_kernel, nodes, spans), grid=(til...  8.3 us
    unnamed x14, local copies, waits for them, and re-layouts  4.55 us
    ppermute x1, starting transfers between devices, per_device(): halo = lax.ppermute(edge, 'ctx', [(i - 1, i) for i in range(1, count)])  4.54 us
    convert_element_type x1, other arithmetic, per_device(): edge = (mr_qkv[rows - LEN:, channels:2 * channels].astype(F32) * mr_qkv[r...  1.79 us
  transfers between devices with their start and end apart: 1, of which 1 were waited for; matrix products, arithmetic and copies ran while one was open for 1% of the time, Pallas kernels for 11%

profile of v2, /device:TPU:1, one launch (start us, length us, event | category | flops | bytes accessed | tf_op | source)
XLA Modules:
  0.0 74.1 jit_solution(7091222335444823020)
XLA Ops:
  0.0 1.8 %multiply_convert_fusion = bf16[128,4096]{1,0:T(8,128)(2,1)S(1)} fusion(bf16[512,12288]{1,0:T(8,128)(2,1)} %refs_2_.1), kind=kLoop, calls=%fused_computation | loop fusion | flops 2097152 | bytes 3145728 | tf_op jit(solution)/shard_map/convert_element_type | solution.py:318
  1.8 4.5 %collective-permute-start = (bf16[128,4096]{1,0:T(8,128)(2,1)S(1)}, bf16[128,4096]{1,0:T(8,128)(2,1)S(1)}, u32[]{:S(2)}, u32[]{:S(2)}) collective-permute-start(bf16[128,4096]{1,0:T(8,128)(2,1)S(1)} %multiply_convert_fusion), channel_id=1, source_target_pairs={{0,1},{1,2},{2,3},{3,4},{4,5},{5,6},{6,7},{7,8},{8,9},{9,10},{10,1... | collective-permute-start | bytes 3145736 | tf_op jit(solution)/shard_map/ppermute | solution.py:319
  6.3 1.1 %pad_maximum_fusion.modal_ref.refs_5_.decay_ref = f32[32,4096]{1,0:T(8,128)S(1)} fusion(f32[16,4096]{1,0:T(8,128)} %bitcast.2, f32[16,4096]{1,0:T(8,128)} %bitcast.3), kind=kLoop, calls=%fused_computation.1 | loop fusion | flops 131072 | bytes 1048576 | tf_op jit(solution)/shard_map/concatenate | solution.py:320
  7.4 0.0 copy-start.2
  7.4 1.0 %copy-done.2 = bf16[800,256]{1,0:T(8,128)(2,1)S(1)} copy-done((bf16[800,256]{1,0:T(8,128)(2,1)S(1)}, bf16[800,256]{1,0:T(8,128)(2,1)}, u32[]{:S(2)}) %copy-start.2) | copy-done | bytes 409624
  8.4 0.0 copy-start.6
  8.4 0.8 %copy-done.6 = bf16[256,128]{1,0:T(8,128)(2,1)S(1)} copy-done((bf16[256,128]{1,0:T(8,128)(2,1)S(1)}, bf16[256,128]{1,0:T(8,128)(2,1)}, u32[]{:S(2)}) %copy-start.6) | copy-done | bytes 65560
  9.3 0.0 copy-start
  9.3 8.3 %prepare.1.refs_6_.node_ref = f32[1024,4096]{1,0:T(8,128)} custom-call(bf16[256,128]{1,0:T(8,128)(2,1)S(1)} %copy-done.6, f32[32,4096]{1,0:T(8,128)S(1)} %pad_maximum_fusion.modal_ref.refs_5_.decay_ref, bf16[800,256]{1,0:T(8,128)(2,1)S(1)} %copy-done.2), custom_call_target="tpu_custom_call" | custom-call | tf_op jit(solution)/shard_map/prepare/pallas_call | solution.py:331
  17.6 0.0 copy-start.3
  17.6 0.5 collective-permute-done.refs_3_
  18.1 0.0 copy-done
  18.1 23.1 %near.1 = (f32[512,4096]{1,0:T(8,128)}, f32[16,4096]{1,0:T(8,128)S(1)}) custom-call(bf16[512,12288]{1,0:T(8,128)(2,1)} %refs_2_.1, bf16[512,12288]{1,0:T(8,128)(2,1)} %refs_2_.1, bf16[512,12288]{1,0:T(8,128)(2,1)} %refs_2_.1, bf16[128,4096]{1,0:T(8,128)(2,1)S(1)} %collective-permute-done.refs_3_, bf16[512,8192]{1,0:T(8,128)(2,1)} %query_ref.1, ...), custom_call_target="tpu_custom_call" | custom-call | tf_op jit(solution)/shard_map/near/pallas_call | solution.py:342
  41.2 0.0 copy-start.5
  41.2 0.7 copy-done.5
  41.9 19.7 %exchange.1.state_ref = f32[16,4096]{1,0:T(8,128)} custom-call(f32[16,4096]{1,0:T(8,128)} %copy-done.5, f32[32,4096]{1,0:T(8,128)} %copy-done), custom_call_target="tpu_custom_call" | custom-call | tf_op jit(solution)/shard_map/exchange/pallas_call | solution.py:357
  61.6 0.0 copy-done.3
  61.6 0.0 copy-start.1
  61.6 1.0 %copy-done.1 = f32[32,4096]{1,0:T(8,128)S(1)} copy-done((f32[32,4096]{1,0:T(8,128)S(1)}, f32[32,4096]{1,0:T(8,128)}, u32[]{:S(2)}) %copy-start.1) | copy-done | bytes 524312
  62.6 0.0 copy-start.4
  62.6 0.9 %copy-done.4 = f32[16,4096]{1,0:T(8,128)S(1)} copy-done((f32[16,4096]{1,0:T(8,128)S(1)}, f32[16,4096]{1,0:T(8,128)}, u32[]{:S(2)}) %copy-start.4) | copy-done | bytes 262168
  63.6 10.5 %far.1 = bf16[512,4096]{1,0:T(8,128)(2,1)} custom-call(f32[512,4096]{1,0:T(8,128)} %get-tuple-element.7.value_ref, bf16[512,8192]{1,0:T(8,128)(2,1)} %query_ref.1, f32[16,4096]{1,0:T(8,128)S(1)} %copy-done.4, f32[32,4096]{1,0:T(8,128)S(1)} %copy-done.1, f32[1024,4096]{1,0:T(8,128)} %prepare.1.refs_6_.node_ref, bf16[800,256]{1,0:T(8,128)(2,1)S(1)} %copy-done.3), custom_call_target="tpu_custom_call" | custom-call | tf_op jit(solution)/shard_map/far/pallas_call | solution.py:370
Async XLA Ops:
  1.8 16.3 %collective-permute-start = (bf16[128,4096]{1,0:T(8,128)(2,1)S(1)}, bf16[128,4096]{1,0:T(8,128)(2,1)S(1)}, u32[]{:S(2)}, u32[]{:S(2)}) collective-permute-start(bf16[128,4096]{1,0:T(8,128)(2,1)S(1)} %multiply_convert_fusion), channel_id=1, source_target_pairs={{0,1},{1,2},{2,3},{3,4},{4,5},{5,6},{6,7},{7,8},{8,9},{9,10},{10,1... | collective-permute-start | bytes 3145736 | tf_op jit(solution)/shard_map/ppermute | solution.py:319
  7.4 1.0 %copy-start.2 = (bf16[800,256]{1,0:T(8,128)(2,1)S(1)}, bf16[800,256]{1,0:T(8,128)(2,1)}, u32[]{:S(2)}) copy-start(bf16[800,256]{1,0:T(8,128)(2,1)} %constant.2.clone.packed_ref.refs_7_) | copy-start | bytes 1228804
  8.4 0.8 %copy-start.6 = (bf16[256,128]{1,0:T(8,128)(2,1)S(1)}, bf16[256,128]{1,0:T(8,128)(2,1)}, u32[]{:S(2)}) copy-start(bf16[256,128]{1,0:T(8,128)(2,1)} %filt_ref.1) | copy-start | bytes 196612
  9.3 8.8 %copy-start = (f32[32,4096]{1,0:T(8,128)}, f32[32,4096]{1,0:T(8,128)S(1)}, u32[]{:S(2)}) copy-start(f32[32,4096]{1,0:T(8,128)S(1)} %pad_maximum_fusion.modal_ref.refs_5_.decay_ref) | copy-start | bytes 1572868
  17.6 44.0 %copy-start.3 = (bf16[800,256]{1,0:T(8,128)(2,1)S(1)}, bf16[800,256]{1,0:T(8,128)(2,1)}, u32[]{:S(2)}) copy-start(bf16[800,256]{1,0:T(8,128)(2,1)} %constant.2.clone.packed_ref.refs_7_) | copy-start | bytes 1228804
  41.2 0.7 copy-start.5
  61.6 1.0 %copy-start.1 = (f32[32,4096]{1,0:T(8,128)S(1)}, f32[32,4096]{1,0:T(8,128)}, u32[]{:S(2)}) copy-start(f32[32,4096]{1,0:T(8,128)} %copy-done) | copy-start | bytes 1572868
  62.6 0.9 %copy-start.4 = (f32[16,4096]{1,0:T(8,128)S(1)}, f32[16,4096]{1,0:T(8,128)}, u32[]{:S(2)}) copy-start(f32[16,4096]{1,0:T(8,128)} %exchange.1.state_ref) | copy-start | bytes 786436

commit v3 on v2

--- a/solution.py
+++ b/solution.py
@@ -138,7 +138,7 @@
 
 def near_chunk(
     spans, q_ref, k_ref, v_ref, halo_ref, key_ref, modal_ref, prepared_ref, packed_ref,
-    out_ref, sum_ref,
+    out_ref,
 ):
     blocks = q_ref.shape[0] // LEN
     half = LEN // 2
@@ -196,115 +196,129 @@
             part = weights * seen[i][2 * LEN + k : 2 * LEN + k + 1]
             ended = part if ended is None else ended + part
         state = ended if state is None else step * state + ended
-    sum_ref[...] = state
-
-
-def near_kernel(spans, *refs):
-    packed_ref = refs[7]
-    for i in range(refs[0].shape[1] // CHUNK):
-        cut = lambda ref: ref.at[:, i * CHUNK : (i + 1) * CHUNK]
-        parts = [ref if ref is packed_ref else cut(ref) for ref in refs]
-        near_chunk(spans, *parts)
-
-
-def far_kernel(spans, value_ref, query_ref, state_ref, modal_ref, node_ref, packed_ref, out_ref):
+    return state
+
+
+def far_tile(spans, value_ref, query_ref, state, modal_ref, node_ref, packed_ref, out_ref):
     modes = modal_ref.shape[0] // 2
     decay = modal_ref[:modes, :]
     near = table_at(packed_ref, spans[2])
     step = jnp.exp(-np.float32(LEN) * decay)
-    start = modal_ref[modes:, :] * jnp.exp(-decay) * state_ref[...]
-    for i in range(value_ref.shape[0] // LEN):
+    start = modal_ref[modes:, :] * jnp.exp(-decay) * state
+    for i in range(query_ref.shape[0] // LEN):
         rows = pl.ds(i * LEN, LEN)
         long_conv = value_ref[rows, :] + dot(near, tripled(weighted(node_ref, 0, start)))
         out_ref[rows, :] = (query_ref[rows, :].astype(F32) * long_conv).astype(BF16)
         start = step * start
 
 
-def exchange_kernel(
-    count, tokens, ended_ref, decay_ref, out_ref, got, starts, landed,
+def main_kernel(
+    spans, count, tiles, q_ref, k_ref, v_ref, halo_ref, key_ref, modal_ref, prepared_ref,
+    packed_ref, all_ref, query_ref, node_ref, out_ref, values, ended, got, starts, landed,
     send_one, recv_one, send_two, recv_two,
 ):
+    turn_now = pl.program_id(0)
     mine = lax.axis_index("ctx")
-    share = got.shape[2]
-
-    def other(k):
-        return lax.rem(mine + k, count)
-
-    def columns(k):
-        return pl.ds(pl.multiple_of(k * share, share), share)
-
-    def first(k):
+    tokens, width = q_ref.shape
+    modes, share = got.shape[1:]
+    per = width // share
+
+    def copy(source, target, send, recv, slot, k):
         return pltpu.make_async_remote_copy(
-            src_ref=ended_ref.at[:, columns(k)],
-            dst_ref=got.at[mine],
-            send_sem=send_one.at[k],
-            recv_sem=recv_one.at[mine],
+            src_ref=source.at[k],
+            dst_ref=target.at[slot],
+            send_sem=send.at[k],
+            recv_sem=recv.at[slot],
             device_id={"ctx": k},
             device_id_type=pl.DeviceIdType.MESH,
         )
 
+    def first(k):
+        return copy(ended, got, send_one, recv_one, mine, k)
+
+    def second(k):
+        return copy(starts, landed, send_two, recv_two, mine, k)
+
     def arrived(buffer, sem, k):
-        return pltpu.make_async_remote_copy(
-            src_ref=buffer.at[k],
-            dst_ref=buffer.at[k],
-            send_sem=sem.at[k],
-            recv_sem=sem.at[k],
-            device_id={"ctx": k},
-            device_id_type=pl.DeviceIdType.MESH,
+        return copy(buffer, buffer, sem, sem, k, k)
+
+    def other(k):
+        return lax.rem(mine + k, count)
+
+    @pl.when(turn_now == 0)
+    def _():
+        barrier = pltpu.get_barrier_semaphore()
+
+        @pl.loop(1, count)
+        def _(k):
+            pl.semaphore_signal(
+                barrier, inc=1, device_id={"ctx": other(k)}, device_id_type=pl.DeviceIdType.MESH
+            )
+
+        pl.semaphore_wait(barrier, count - 1)
+
+    @pl.when(turn_now < tiles)
+    def _():
+        refs = [q_ref, k_ref, v_ref, halo_ref, key_ref, modal_ref, prepared_ref]
+        states = []
+        for i in range(width // CHUNK):
+            columns = slice(i * CHUNK, (i + 1) * CHUNK)
+            parts = [ref.at[:, columns] for ref in refs]
+            states.append(
+                near_chunk(spans, *parts, packed_ref, values.at[turn_now, :, columns])
+            )
+        state = jnp.concatenate(states, axis=1)
+        for i in range(per):
+            owner = turn_now * per + i
+            ended[owner] = state[:, i * share : (i + 1) * share]
+
+            @pl.when(owner != mine)
+            def _():
+                first(owner).start()
+
+    last = tiles - 1
+    own = lax.div(mine, per)
+
+    @pl.when((turn_now == own + 1) & (own < last) | (turn_now == last) & (own == last))
+    def _():
+        columns = pl.ds(pl.multiple_of(mine * share, share), share)
+        own_decay = jnp.exp(-np.float32(tokens) * all_ref[:modes, columns])
+        got[mine] = ended[mine]
+
+        def turn(k, running):
+            starts[k] = running
+
+            @pl.when(k != mine)
+            def _():
+                second(k).start()
+                arrived(got, recv_one, k).wait_recv()
+
+            return own_decay * running + got[k]
+
+        lax.fori_loop(0, count, turn, jnp.zeros((modes, share), F32))
+        landed[mine] = starts[mine]
+
+    @pl.when(turn_now >= tiles)
+    def _():
+        tile = turn_now - tiles
+        for i in range(per):
+            owner = tile * per + i
+
+            @pl.when(owner != mine)
+            def _():
+                arrived(landed, recv_two, owner).wait_recv()
+
+        state = jnp.concatenate([landed[tile * per + i] for i in range(per)], axis=1)
+        far_tile(
+            spans, values.at[tile], query_ref, state, modal_ref, node_ref, packed_ref, out_ref
         )
 
-    def second(k):
-        return pltpu.make_async_remote_copy(
-            src_ref=starts.at[k],
-            dst_ref=landed.at[mine],
-            send_sem=send_two.at[k],
-            recv_sem=recv_two.at[mine],
-            device_id={"ctx": k},
-            device_id_type=pl.DeviceIdType.MESH,
-        )
-
-    barrier = pltpu.get_barrier_semaphore()
-
-    @pl.loop(1, count)
-    def _(k):
-        pl.semaphore_signal(
-            barrier, inc=1, device_id={"ctx": other(k)}, device_id_type=pl.DeviceIdType.MESH
-        )
-
-    pl.semaphore_wait(barrier, count - 1)
-
-    @pl.loop(1, count)
-    def _(k):
-        first(other(k)).start()
-
-    got[mine] = ended_ref[:, columns(mine)]
-    own_decay = jnp.exp(-np.float32(tokens) * decay_ref[: got.shape[1], columns(mine)])
-
-    def turn(k, running):
-        starts[k] = running
-
-        @pl.when(k != mine)
-        def _():
-            second(k).start()
-            arrived(got, recv_one, k).wait_recv()
-
-        return own_decay * running + got[k]
-
-    lax.fori_loop(0, count, turn, jnp.zeros(own_decay.shape, F32))
-    landed[mine] = starts[mine]
-
-    @pl.loop(1, count)
-    def _(k):
-        arrived(landed, recv_two, other(k)).wait_recv()
-
-    @pl.loop(0, count)
-    def _(k):
-        out_ref[:, columns(k)] = landed[k]
-
-    @pl.loop(1, count)
-    def _(k):
-        first(other(k)).wait_send()
-        second(other(k)).wait_send()
+    @pl.when(turn_now == 2 * tiles - 1)
+    def _():
+        @pl.loop(1, count)
+        def _(k):
+            first(other(k)).wait_send()
+            second(other(k)).wait_send()
 
 
 def per_device(mr_qkv, mr_filter, li_gates, decay, residue):
@@ -339,45 +353,38 @@
         compiler_params=params,
         name="prepare",
     )(mr_filter, modal, packed)
-    values, ended = pl.pallas_call(
-        functools.partial(near_kernel, spans),
-        grid=(tiles,),
-        in_specs=[
-            part(rows, 0), part(rows, 1), part(rows, 2), part(LEN), part(rows, 1),
-            part(2 * modes), part(height), whole(packed),
-        ],
-        out_specs=[part(rows), part(modes)],
-        out_shape=[shape(rows), shape(modes)],
-        compiler_params=params,
-        name="near",
-    )(mr_qkv, mr_qkv, mr_qkv, halo, li_gates, modal, prepared, packed)
+    def held(height, k=0):
+        def place(j):
+            return 0, k * tiles + j - lax.div(j, tiles) * (j - tiles + 1)
+
+        return pl.BlockSpec((height, width), place)
+
+    def later(height, k=0):
+        return pl.BlockSpec((height, width), lambda j: (k, lax.div(j, tiles) * (j - tiles)))
 
     share = channels // count
     slots = pltpu.VMEM((count, modes, share), F32)
-    incoming = pl.pallas_call(
-        functools.partial(exchange_kernel, count, rows),
-        in_specs=[pl.BlockSpec(memory_space=pltpu.VMEM)] * 2,
-        out_specs=pl.BlockSpec(memory_space=pltpu.VMEM),
-        out_shape=shape(modes),
-        scratch_shapes=[slots] * 3 + [pltpu.SemaphoreType.DMA((count,))] * 4,
-        compiler_params=pltpu.CompilerParams(collective_id=0, has_side_effects=True),
-        name="exchange",
-    )(ended, modal)
-
-    node_part = pl.BlockSpec(
-        (modes * NODES, width), lambda j: (4 * LEN // (modes * NODES), j)
-    )
     return pl.pallas_call(
-        functools.partial(far_kernel, spans),
-        grid=(tiles,),
+        functools.partial(main_kernel, spans, count, tiles),
+        grid=(2 * tiles,),
         in_specs=[
-            part(rows), part(rows), part(modes), part(2 * modes), node_part, whole(packed)
+            held(rows, 0), held(rows, 1), held(rows, 2), held(LEN), held(rows, 1),
+            pl.BlockSpec((2 * modes, width), lambda j: (0, lax.rem(j, tiles))),
+            held(height), whole(packed), whole(modal), later(rows),
+            later(modes * NODES, 4 * LEN // (modes * NODES)),
         ],
-        out_specs=part(rows),
+        out_specs=later(rows),
         out_shape=jax.ShapeDtypeStruct((rows, channels), BF16),
-        compiler_params=params,
-        name="far",
-    )(values, li_gates, incoming, modal, prepared, packed)
+        scratch_shapes=[pltpu.VMEM((tiles, rows, width), F32)]
+        + [slots] * 4
+        + [pltpu.SemaphoreType.DMA((count,))] * 4,
+        compiler_params=pltpu.CompilerParams(
+            vmem_limit_bytes=52 * 2**20, collective_id=0, has_side_effects=True
+        ),
+        name="main",
+    )(
+        mr_qkv, mr_qkv, mr_qkv, halo, li_gates, modal, prepared, packed, modal, li_gates, prepared
+    )
 
 
 def solution(mesh):

time: 74.6 us -> 66.3 us (0.89)
  the two profiles are of different devices: /device:TPU:1 before, /device:TPU:29 now
where the time goes in v3:
time: 66.3 us; the launch traced here: 65.9 us
  Pallas kernels  57 us (86%)
  local copies, waits for them, and re-layouts  4.71 us (7%)
  other arithmetic  2.91 us (4%)
  starting transfers between devices  1.29 us (2%)
    pallas_call x1, Pallas kernels, per_device(): pl.pallas_call(functools.partial(main_kernel, spans, count, tiles), grid=...  48.7 us
    pallas_call x1, Pallas kernels, per_device(): pl.pallas_call(functools.partial(prepare_kernel, nodes, spans), grid=(til...  8.25 us
    unnamed x5, local copies, waits for them, and re-layouts  4.71 us
    convert_element_type x1, other arithmetic, per_device(): edge = (mr_qkv[rows - LEN:, channels:2 * channels].astype(F32) * mr_qkv[r...  1.84 us
  transfers between devices with their start and end apart: 1, of which 0 were waited for; matrix products, arithmetic and copies ran while one was open for 2% of the time, Pallas kernels for 13%

profile of v3, /device:TPU:29, one launch (start us, length us, event | category | flops | bytes accessed | tf_op | source)
XLA Modules:
  0.0 65.9 jit_solution(1408480267215336372)
XLA Ops:
  0.0 0.0 copy-start
  0.0 0.0 copy-start.1
  0.0 1.8 %multiply_convert_fusion = bf16[128,4096]{1,0:T(8,128)(2,1)S(1)} fusion(bf16[512,12288]{1,0:T(8,128)(2,1)} %v_ref.1), kind=kLoop, calls=%fused_computation | loop fusion | flops 2097152 | bytes 3145728 | tf_op jit(solution)/shard_map/convert_element_type | solution.py:332
  1.9 1.3 %collective-permute-start = (bf16[128,4096]{1,0:T(8,128)(2,1)S(1)}, bf16[128,4096]{1,0:T(8,128)(2,1)S(1)}, u32[]{:S(2)}, u32[]{:S(2)}) collective-permute-start(bf16[128,4096]{1,0:T(8,128)(2,1)S(1)} %multiply_convert_fusion), channel_id=1, source_target_pairs={{0,1},{1,2},{2,3},{3,4},{4,5},{5,6},{6,7},{7,8},{8,9},{9,10},{10,1... | collective-permute-start | bytes 3145736 | tf_op jit(solution)/shard_map/ppermute | solution.py:333
  3.2 1.1 %pad_maximum_fusion.modal_ref.all_ref = f32[32,4096]{1,0:T(8,128)S(1)} fusion(f32[16,4096]{1,0:T(8,128)} %bitcast.2, f32[16,4096]{1,0:T(8,128)} %bitcast.3), kind=kLoop, calls=%fused_computation.1 | loop fusion | flops 131072 | bytes 1048576 | tf_op jit(solution)/shard_map/concatenate | solution.py:334
  4.2 0.0 copy-done
  4.2 0.0 copy-done.1
  4.2 8.2 %prepare.1.prepared_ref.node_ref = f32[1024,4096]{1,0:T(8,128)} custom-call(bf16[256,128]{1,0:T(8,128)(2,1)S(1)} %copy-done.1, f32[32,4096]{1,0:T(8,128)S(1)} %pad_maximum_fusion.modal_ref.all_ref, bf16[800,256]{1,0:T(8,128)(2,1)S(1)} %copy-done), custom_call_target="tpu_custom_call" | custom-call | tf_op jit(solution)/shard_map/prepare/pallas_call | solution.py:345
  12.5 0.0 collective-permute-done.halo_ref
  12.5 48.7 %main.1 = bf16[512,4096]{1,0:T(8,128)(2,1)} custom-call(bf16[512,12288]{1,0:T(8,128)(2,1)} %v_ref.1, bf16[512,12288]{1,0:T(8,128)(2,1)} %v_ref.1, bf16[512,12288]{1,0:T(8,128)(2,1)} %v_ref.1, bf16[128,4096]{1,0:T(8,128)(2,1)S(1)} %collective-permute-done.halo_ref, bf16[512,8192]{1,0:T(8,128)(2,1)} %query_ref.1, ...), custom_call_target="tpu_custom_call" | custom-call | tf_op jit(solution)/shard_map/main/pallas_call | solution.py:367
  61.2 4.7 %copy.8 = bf16[512,4096]{1,0:T(8,128)(2,1)} copy(bf16[512,4096]{1,0:T(8,128)(2,1)} %main.1) | data formatting | bytes 8388608
Async XLA Ops:
  0.0 4.2 %copy-start = (bf16[800,256]{1,0:T(8,128)(2,1)S(1)}, bf16[800,256]{1,0:T(8,128)(2,1)}, u32[]{:S(2)}) copy-start(bf16[800,256]{1,0:T(8,128)(2,1)} %constant.2.clone.packed_ref) | copy-start | bytes 1228804
  0.0 4.2 %copy-start.1 = (bf16[256,128]{1,0:T(8,128)(2,1)S(1)}, bf16[256,128]{1,0:T(8,128)(2,1)}, u32[]{:S(2)}) copy-start(bf16[256,128]{1,0:T(8,128)(2,1)} %filt_ref.1) | copy-start | bytes 196612
  1.9 10.6 %collective-permute-start = (bf16[128,4096]{1,0:T(8,128)(2,1)S(1)}, bf16[128,4096]{1,0:T(8,128)(2,1)S(1)}, u32[]{:S(2)}, u32[]{:S(2)}) collective-permute-start(bf16[128,4096]{1,0:T(8,128)(2,1)S(1)} %multiply_convert_fusion), channel_id=1, source_target_pairs={{0,1},{1,2},{2,3},{3,4},{4,5},{5,6},{6,7},{7,8},{8,9},{9,10},{10,1... | collective-permute-start | bytes 3145736 | tf_op jit(solution)/shard_map/ppermute | solution.py:333

commit v4 on v3

--- a/solution.py
+++ b/solution.py
@@ -276,10 +276,9 @@
             def _():
                 first(owner).start()
 
-    last = tiles - 1
     own = lax.div(mine, per)
 
-    @pl.when((turn_now == own + 1) & (own < last) | (turn_now == last) & (own == last))
+    @pl.when(turn_now == own + 3)
     def _():
         columns = pl.ds(pl.multiple_of(mine * share, share), share)
         own_decay = jnp.exp(-np.float32(tokens) * all_ref[:modes, columns])

time: 66.3 us -> 62.1 us (0.937)
  the two profiles are of different devices: /device:TPU:29 before, /device:TPU:1 now
where the time goes in v4:
time: 62.1 us; the launch traced here: 61.2 us
  Pallas kernels  46.6 us (75%)
  local copies, waits for them, and re-layouts  4.71 us (8%)
  starting transfers between devices  4.54 us (7%)
  other arithmetic  2.91 us (5%)
  waiting for transfers between devices  2.39 us (4%)
    pallas_call x1, Pallas kernels, per_device(): pl.pallas_call(functools.partial(main_kernel, spans, count, tiles), grid=...  38.4 us
    pallas_call x1, Pallas kernels, per_device(): pl.pallas_call(functools.partial(prepare_kernel, nodes, spans), grid=(til...  8.25 us
    unnamed x5, local copies, waits for them, and re-layouts  4.71 us
    ppermute x1, starting transfers between devices, per_device(): halo = lax.ppermute(edge, 'ctx', [(i - 1, i) for i in range(1, count)])  4.54 us
    ppermute x1, waiting for transfers between devices, per_device(): halo = lax.ppermute(edge, 'ctx', [(i - 1, i) for i in range(1, count)])  2.39 us
    convert_element_type x1, other arithmetic, per_device(): edge = (mr_qkv[rows - LEN:, channels:2 * channels].astype(F32) * mr_qkv[r...  1.84 us
  transfers between devices with their start and end apart: 1, of which 1 were waited for; matrix products, arithmetic and copies ran while one was open for 2% of the time, Pallas kernels for 13%

profile of v4, /device:TPU:1, one launch (start us, length us, event | category | flops | bytes accessed | tf_op | source)
XLA Modules:
  0.0 61.2 jit_solution(17966054114010104672)
XLA Ops:
  0.0 0.0 copy-start
  0.0 0.0 copy-start.1
  0.0 1.8 %multiply_convert_fusion = bf16[128,4096]{1,0:T(8,128)(2,1)S(1)} fusion(bf16[512,12288]{1,0:T(8,128)(2,1)} %v_ref.1), kind=kLoop, calls=%fused_computation | loop fusion | flops 2097152 | bytes 3145728 | tf_op jit(solution)/shard_map/convert_element_type | solution.py:331
  1.9 4.5 %collective-permute-start = (bf16[128,4096]{1,0:T(8,128)(2,1)S(1)}, bf16[128,4096]{1,0:T(8,128)(2,1)S(1)}, u32[]{:S(2)}, u32[]{:S(2)}) collective-permute-start(bf16[128,4096]{1,0:T(8,128)(2,1)S(1)} %multiply_convert_fusion), channel_id=1, source_target_pairs={{0,1},{1,2},{2,3},{3,4},{4,5},{5,6},{6,7},{7,8},{8,9},{9,10},{10,1... | collective-permute-start | bytes 3145736 | tf_op jit(solution)/shard_map/ppermute | solution.py:332
  6.4 1.1 %pad_maximum_fusion.modal_ref.all_ref = f32[32,4096]{1,0:T(8,128)S(1)} fusion(f32[16,4096]{1,0:T(8,128)} %bitcast.2, f32[16,4096]{1,0:T(8,128)} %bitcast.3), kind=kLoop, calls=%fused_computation.1 | loop fusion | flops 131072 | bytes 1048576 | tf_op jit(solution)/shard_map/concatenate | solution.py:333
  7.5 0.0 copy-done
  7.5 0.0 copy-done.1
  7.5 8.2 %prepare.1.prepared_ref.node_ref = f32[1024,4096]{1,0:T(8,128)} custom-call(bf16[256,128]{1,0:T(8,128)(2,1)S(1)} %copy-done.1, f32[32,4096]{1,0:T(8,128)S(1)} %pad_maximum_fusion.modal_ref.all_ref, bf16[800,256]{1,0:T(8,128)(2,1)S(1)} %copy-done), custom_call_target="tpu_custom_call" | custom-call | tf_op jit(solution)/shard_map/prepare/pallas_call | solution.py:344
  15.7 2.4 %collective-permute-done.halo_ref = bf16[128,4096]{1,0:T(8,128)(2,1)S(1)} collective-permute-done((bf16[128,4096]{1,0:T(8,128)(2,1)S(1)}, bf16[128,4096]{1,0:T(8,128)(2,1)S(1)}, u32[]{:S(2)}, u32[]{:S(2)}) %collective-permute-start) | collective-permute-done | bytes 1048608 | tf_op jit(solution)/shard_map/ppermute | solution.py:332
  18.1 38.4 %main.1 = bf16[512,4096]{1,0:T(8,128)(2,1)} custom-call(bf16[512,12288]{1,0:T(8,128)(2,1)} %v_ref.1, bf16[512,12288]{1,0:T(8,128)(2,1)} %v_ref.1, bf16[512,12288]{1,0:T(8,128)(2,1)} %v_ref.1, bf16[128,4096]{1,0:T(8,128)(2,1)S(1)} %collective-permute-done.halo_ref, bf16[512,8192]{1,0:T(8,128)(2,1)} %query_ref.1, ...), custom_call_target="tpu_custom_call" | custom-call | tf_op jit(solution)/shard_map/main/pallas_call | solution.py:366
  56.5 4.7 %copy.8 = bf16[512,4096]{1,0:T(8,128)(2,1)} copy(bf16[512,4096]{1,0:T(8,128)(2,1)} %main.1) | data formatting | bytes 8388608
Async XLA Ops:
  0.0 7.5 %copy-start = (bf16[800,256]{1,0:T(8,128)(2,1)S(1)}, bf16[800,256]{1,0:T(8,128)(2,1)}, u32[]{:S(2)}) copy-start(bf16[800,256]{1,0:T(8,128)(2,1)} %constant.2.clone.packed_ref) | copy-start | bytes 1228804
  0.0 7.5 %copy-start.1 = (bf16[256,128]{1,0:T(8,128)(2,1)S(1)}, bf16[256,128]{1,0:T(8,128)(2,1)}, u32[]{:S(2)}) copy-start(bf16[256,128]{1,0:T(8,128)(2,1)} %filt_ref.1) | copy-start | bytes 196612
  1.9 16.3 %collective-permute-start = (bf16[128,4096]{1,0:T(8,128)(2,1)S(1)}, bf16[128,4096]{1,0:T(8,128)(2,1)S(1)}, u32[]{:S(2)}, u32[]{:S(2)}) collective-permute-start(bf16[128,4096]{1,0:T(8,128)(2,1)S(1)} %multiply_convert_fusion), channel_id=1, source_target_pairs={{0,1},{1,2},{2,3},{3,4},{4,5},{5,6},{6,7},{7,8},{8,9},{9,10},{10,1... | collective-permute-start | bytes 3145736 | tf_op jit(solution)/shard_map/ppermute | solution.py:332
